TPU v7x, 32 devices: a whole 2x2x4 slice. The times are simulated.
32 devices in a mesh: filt: 16 (over z, y, x), slab: 2 (over core).
Axes of the slice: x: 2, y: 2, z: 4, core: 2. Of those that a mesh axis runs over, the one named last changes fastest.
Arguments:
- activations: bfloat16 [512, 4, 512], P('filt', 'slab'), may hold values from -6 to 6
- grad_out: bfloat16 [512, 4, 512], P('filt', 'slab'), may hold values from -6 to 6
- weights: bfloat16 [27, 256, 256], P(None, 'filt'), may hold values from -0.078125 to 0.078125
Outputs:
- out_map: bfloat16 [512, 4, 512], P('filt', 'slab')
- grad_in: bfloat16 [512, 4, 512], P('filt', 'slab')
- filter_grad: float32 [27, 256, 256], P(None, 'filt')
All inputs are finite; a program needn't handle non-finite values.
Results may differ from a plain program's by a relative error of at most 0.001.
Values may be sent and summed in bfloat16 or wider, within the bound.
A program may use at most 64 MiB of HBM per device.

v0:
```python
import math

import jax
import jax.numpy as jnp
from jax import lax
from jax.experimental import pallas as pl
from jax.experimental.pallas import tpu as pltpu
from jax.sharding import PartitionSpec as P

CH_IN = 256
CH_OUT = 256
GROUPS = 8
ROWS = 8
WIDTH = 64


def extended(shard, sides, width):
    for axis, dim in sides:
        count, length = (lax.axis_size(axis), shard.shape[dim])
        up = [(i, (i + 1) % count) for i in range(count - 1)]
        down = [(j, i) for i, j in up]
        last = lax.slice_in_dim(shard, length - width, length, axis=dim)
        initial = lax.slice_in_dim(shard, 0, width, axis=dim)
        before = lax.ppermute(last, axis, up)
        after = lax.ppermute(initial, axis, down)
        shard = jnp.concatenate([before, shard, after], axis=dim)
    return shard


def shifted(block, axis, distance):
    devices = range(lax.axis_size(axis))
    route = [(i - distance, i) for i in devices if i - distance in devices]
    return lax.ppermute(block, axis, route)


def from_partner(value, axis, apart):
    mask = 2**apart
    pairs = [(source, source ^ mask) for source in range(lax.axis_size(axis))]
    return lax.ppermute(value, axis, pairs)


def correlate(image, kernel, lhs_spec):
    return lax.conv_general_dilated(
        image,
        kernel,
        (1, 1, 1),
        ((0, 0), (0, 0), (1, 1)),
        dimension_numbers=(lhs_spec, "OIDHW", "NCDHW"),
        preferred_element_type=jnp.float32,
    )


def pad_block(pieces):
    chan_count = pieces.shape[0]
    depth_dev = pieces.shape[1]
    deepened = extended(pieces, (("slab", 1),), 1)
    planes_grid = deepened.reshape(chan_count, depth_dev + 2, ROWS, WIDTH)
    blocks_all = lax.axis_size("filt") // GROUPS
    row_pos = lax.axis_index("filt") // GROUPS
    from_below = shifted(planes_grid[:, :, ROWS - 1 :], "filt", GROUPS)
    from_above = shifted(planes_grid[:, :, :1], "filt", -GROUPS)
    from_below = jnp.where(row_pos == 0, jnp.zeros_like(from_below), from_below)
    from_above = jnp.where(row_pos == blocks_all - 1, jnp.zeros_like(from_above), from_above)
    return jnp.concatenate([from_below, planes_grid, from_above], axis=2)


def gather_groups(pieces):
    my_index = lax.axis_index("filt")
    for bit_num in range(GROUPS.bit_length() - 1):
        partner = from_partner(pieces, "filt", bit_num)
        upper_side = my_index // (1 << bit_num) % 2 == 1
        lower_part = jnp.where(upper_side, partner, pieces)
        upper_part = jnp.where(upper_side, pieces, partner)
        pieces = jnp.concatenate([lower_part, upper_part], axis=0)
    return pieces


def gather_blocks(pieces, axis_dim):
    blocks_all = lax.axis_size("filt") // GROUPS
    group_bits = GROUPS.bit_length() - 1
    my_index = lax.axis_index("filt")
    for section_num in range(blocks_all.bit_length() - 1):
        bit_num = group_bits + section_num
        partner = from_partner(pieces, "filt", bit_num)
        upper_side = my_index // (1 << bit_num) % 2 == 1
        lower_part = jnp.where(upper_side, partner, pieces)
        upper_part = jnp.where(upper_side, pieces, partner)
        pieces = jnp.concatenate([lower_part, upper_part], axis=axis_dim)
    return pieces


def reduce_halves(partial_value):
    blocks_all = lax.axis_size("filt") // GROUPS
    bits_count = blocks_all.bit_length() - 1
    group_bits = GROUPS.bit_length() - 1
    my_index = lax.axis_index("filt")
    for section_num in range(bits_count):
        bit_num = group_bits + bits_count - 1 - section_num
        half_size = partial_value.shape[1] // 2
        lower_part = partial_value[:, :half_size]
        upper_part = partial_value[:, half_size:]
        upper_side = my_index // (1 << bit_num) % 2 == 1
        sending = jnp.where(upper_side, lower_part, upper_part)
        keeping = jnp.where(upper_side, upper_part, lower_part)
        partial_value = keeping + from_partner(sending, "filt", bit_num)
    return partial_value


def per_device_general(activations, grad_out, weights):
    chan_local = activations.shape[0]
    depth_dev = activations.shape[1]
    blocks_all = lax.axis_size("filt") // GROUPS
    rows_dev = weights.shape[1]
    depth_all = depth_dev * lax.axis_size("slab")
    height_all = ROWS * blocks_all
    whole_in = gather_groups(pad_block(activations))
    whole_grad = gather_groups(pad_block(grad_out))
    group_weights = gather_blocks(weights, 1)
    reordered = jnp.transpose(
        weights.reshape(27, rows_dev, GROUPS, blocks_all, rows_dev), (0, 1, 3, 2, 4)
    ).reshape(27, rows_dev, CH_IN)
    stored_rows = gather_blocks(
        lax.all_to_all(reordered, "filt", split_axis=2, concat_axis=1, tiled=True), 2
    )
    column_weights = jnp.transpose(
        stored_rows.reshape(27, blocks_all, GROUPS, rows_dev, chan_local), (0, 2, 1, 3, 4)
    ).reshape(27, CH_OUT, chan_local)
    out_kernel = jnp.transpose(group_weights, (1, 2, 0)).reshape(chan_local, CH_IN, 3, 3, 3)
    output_sum = correlate(whole_in[None], out_kernel, "NCDHW")
    grad_kernel = grad_out.reshape(chan_local, 1, depth_dev, ROWS, WIDTH)
    filter_terms = correlate(whole_in[:, None], grad_kernel, "NCDHW")
    filter_part = jnp.transpose(filter_terms.reshape(CH_IN, chan_local, 27), (2, 1, 0))
    in_kernel = jnp.transpose(column_weights[::-1], (2, 1, 0)).reshape(chan_local, CH_OUT, 3, 3, 3)
    input_sum = correlate(whole_grad[None], in_kernel, "NCDHW")
    scale_factor = 1.0 / math.sqrt(depth_all * height_all * WIDTH)
    filter_grad = lax.psum(reduce_halves(filter_part), "slab") * scale_factor
    out_map = output_sum.astype(jnp.bfloat16).reshape(chan_local, depth_dev, ROWS * WIDTH)
    grad_in = input_sum.astype(jnp.bfloat16).reshape(chan_local, depth_dev, ROWS * WIDTH)
    return (out_map, grad_in, filter_grad)


PLANE = ROWS * WIDTH
LOCAL = CH_IN // GROUPS
HALO = 128
MESH = pl.DeviceIdType.MESH


def spread(total, low_from):
    column = lax.broadcasted_iota(jnp.int32, (LOCAL, PLANE), 1) % WIDTH
    first, middle, last = (total[k * LOCAL : (k + 1) * LOCAL] for k in range(3))
    if not low_from:
        first, last = last, first
    up = jnp.where(column == 0, 0.0, pltpu.roll(first, 1, 1))
    down = jnp.where(column == WIDTH - 1, 0.0, pltpu.roll(last, PLANE - 1, 1))
    return up + middle + down


def fused_kernel(
    scale, act, grad, own_w, own_wt, out, gin, fgrad,
    vol_in, vol_grad, halo, halo_own, group_w, column_w, shifts,
    terms, terms_core, cross_out, cross_in, half_own, half_in,
    send, recv,
):
    me = lax.axis_index("filt")
    slab = lax.axis_index("slab")
    block, group = me // GROUPS, me % GROUPS
    other_slab = 1 - slab
    across = (1 - block) * GROUPS + group
    rows = own_w.shape[1]

    def remote(src, dst, sem, filt, core):
        return pltpu.make_async_remote_copy(
            src_ref=src, dst_ref=dst, send_sem=send.at[sem], recv_sem=recv.at[sem],
            device_id=(filt, core), device_id_type=MESH,
        )

    def aligned(index, size):
        return pl.ds(pl.multiple_of(index * size, size), size)

    peers = [block * GROUPS + (group + k) % GROUPS for k in range(1, GROUPS)]
    others = [(me + k) % (2 * GROUPS) for k in range(1, 2 * GROUPS)]
    barrier = pltpu.get_barrier_semaphore()
    for device in others:
        pl.semaphore_signal(barrier, inc=1, device_id=(device, slab), device_id_type=MESH)
    pl.semaphore_signal(barrier, inc=1, device_id=(me, other_slab), device_id_type=MESH)

    channels = aligned(group, LOCAL)
    edge = pl.ds(pl.multiple_of((1 - block) * (PLANE - HALO), HALO), HALO)
    halo_own[0] = act[:, :, edge]
    halo_own[1] = grad[:, :, edge]
    pl.semaphore_wait(barrier, 2 * GROUPS)

    halo_copy = remote(halo_own, halo.at[:, 1:3, channels, :], 0, across, slab)
    halo_copy.start()
    act_copies = [
        remote(act, vol_in.at[1:3, 1, channels, :], 8 + k, peer, slab)
        for k, peer in enumerate(peers)
    ]
    for copy in act_copies:
        copy.start()
    group_copy = remote(own_w, group_w.at[:, aligned(block, rows), :], 22, across, slab)
    group_copy.start()
    grad_copies = [
        remote(grad, vol_grad.at[1:3, 1, channels, :], 15 + k, peer, slab)
        for k, peer in enumerate(peers)
    ]
    for copy in grad_copies:
        copy.start()
    mine = aligned(group * 2 + block, rows)
    column_copies = [
        remote(own_wt.at[device % GROUPS], column_w.at[:, mine, :], 23 + k, device, slab)
        for k, device in enumerate(others)
    ]
    for copy in column_copies:
        copy.start()

    zero_plane = 3 * slab
    vol_in[zero_plane, 1] = jnp.zeros((CH_IN, PLANE), jnp.bfloat16)
    vol_grad[zero_plane, 1] = jnp.zeros((CH_IN, PLANE), jnp.bfloat16)
    halo[:, zero_plane] = jnp.zeros((2, CH_IN, HALO), jnp.bfloat16)
    vol_in[1:3, 1, channels, :] = act[...]
    vol_grad[1:3, 1, channels, :] = grad[...]
    group_w[:, aligned(block, rows), :] = own_w[...]
    column_w[:, mine, :] = own_wt[group]
    column = lax.broadcasted_iota(jnp.int32, (LOCAL, PLANE), 1) % WIDTH
    for depth in range(2):
        value = grad[depth].astype(jnp.float32)
        lower = jnp.where(column == WIDTH - 1, 0.0, pltpu.roll(value, PLANE - 1, 1))
        upper = jnp.where(column == 0, 0.0, pltpu.roll(value, 1, 1))
        shifts[depth, 0:LOCAL] = lower.astype(jnp.bfloat16)
        shifts[depth, LOCAL : 2 * LOCAL] = grad[depth]
        shifts[depth, 2 * LOCAL :] = upper.astype(jnp.bfloat16)

    halo_copy.wait_recv()
    halo_copies = [
        remote(halo.at[:, 1:3, channels, :], halo.at[:, 1:3, channels, :], 1 + k, peer, slab)
        for k, peer in enumerate(peers)
    ]
    for copy in halo_copies:
        copy.start()

    gives, takes = 2 - slab, 3 * slab
    for copy in act_copies:
        copy.wait_recv()
    act_plane = remote(vol_in.at[gives, 1], vol_in.at[takes, 1], 38, me, other_slab)
    act_plane.start()
    for copy in halo_copies:
        copy.wait_recv()
    halo_plane = remote(halo.at[:, gives], halo.at[:, takes], 39, me, other_slab)
    halo_plane.start()

    def shift_rows(volume, which, plane):
        edges = halo[which, plane]
        none = jnp.zeros_like(edges)
        whole = jnp.concatenate(
            [jnp.where(block == 1, edges, none), volume[plane, 1], jnp.where(block == 0, edges, none)],
            axis=1,
        )
        volume[plane, 0] = whole[:, HALO - WIDTH : HALO - WIDTH + PLANE]
        volume[plane, 2] = whole[:, HALO + WIDTH : HALO + WIDTH + PLANE]

    shift_rows(vol_in, 0, 1)
    shift_rows(vol_in, 0, 2)
    act_plane.wait_recv()
    halo_plane.wait_recv()
    shift_rows(vol_in, 0, 0)
    shift_rows(vol_in, 0, 3)

    over_cells = (((1,), (1,)), ((), ()))
    half = CH_IN // 2
    for pair in range(9):
        a, b = pair // 3, pair % 3
        total = sum(
            lax.dot_general(
                shifts[depth], vol_in[depth + a, b], over_cells, preferred_element_type=jnp.float32
            )
            for depth in range(2)
        )
        for c in range(3):
            for dest in range(2):
                low = c * LOCAL + dest * rows
                for side in range(2):
                    terms[side, dest, 3 * pair + c] = total[
                        low : low + rows, side * half : (side + 1) * half
                    ]
    terms_copy = remote(terms.at[other_slab], terms_core, 41, me, other_slab)
    terms_copy.start()

    group_copy.wait_recv()
    for depth in range(2):
        total = jnp.zeros((3 * LOCAL, PLANE), jnp.float32)
        for pair in range(9):
            filters = group_w[3 * pair : 3 * pair + 3].reshape(3 * LOCAL, CH_IN)
            total += jnp.dot(
                filters, vol_in[depth + pair // 3, pair % 3], preferred_element_type=jnp.float32
            )
        out[depth] = spread(total, True).astype(out.dtype)

    terms_copy.wait_recv()
    cross_out[...] = terms[slab, 1 - block] + terms_core[1 - block]
    cross = remote(cross_out, cross_in, 42, across, slab)
    cross.start()

    for copy in grad_copies:
        copy.wait_recv()
    grad_plane = remote(vol_grad.at[gives, 1], vol_grad.at[takes, 1], 40, me, other_slab)
    grad_plane.start()
    shift_rows(vol_grad, 1, 1)
    shift_rows(vol_grad, 1, 2)
    grad_plane.wait_recv()
    shift_rows(vol_grad, 1, 0)
    shift_rows(vol_grad, 1, 3)
    for copy in column_copies:
        copy.wait_recv()
    over_rows = (((0,), (0,)), ((), ()))
    totals = [jnp.zeros((HALO, PLANE), jnp.float32) for _ in range(2)]
    for pair in range(9):
        filters = column_w[pair]
        for depth in range(2):
            totals[depth] += lax.dot_general(
                filters, vol_grad[depth + 2 - pair // 3, 2 - pair % 3], over_rows,
                preferred_element_type=jnp.float32,
            )
    for depth in range(2):
        gin[depth] = spread(totals[depth], False).astype(gin.dtype)

    cross.wait_recv()
    half_own[...] = (terms[slab, block] + terms_core[block] + cross_in[...]) * scale
    share = remote(half_own, half_in, 43, me, other_slab)
    share.start()
    fgrad[:, :, aligned(slab, half)] = half_own[...]
    share.wait_recv()
    fgrad[:, :, aligned(other_slab, half)] = half_in[...]

    for copy in (
        [halo_copy, group_copy, act_plane, halo_plane, grad_plane, terms_copy, cross, share]
        + halo_copies + act_copies + grad_copies + column_copies
    ):
        copy.wait_send()


def per_device_paired(activations, grad_out, weights):
    depth_dev = activations.shape[1]
    rows = weights.shape[1]
    cells = depth_dev * 2 * ROWS * 2 * WIDTH
    packed = jnp.transpose(
        weights.reshape(9, 3, rows, GROUPS, LOCAL), (3, 0, 2, 1, 4)
    ).reshape(GROUPS, 9, rows, 3 * LOCAL)
    packed = jnp.pad(packed, ((0, 0), (0, 0), (0, 0), (0, HALO - 3 * LOCAL)))
    vmem = pl.BlockSpec(memory_space=pltpu.VMEM)
    half = CH_IN // 2
    out, gin, fgrad = pl.pallas_call(
        lambda *refs: fused_kernel(1.0 / math.sqrt(cells), *refs),
        out_shape=(
            jax.ShapeDtypeStruct((depth_dev, LOCAL, PLANE), jnp.bfloat16),
            jax.ShapeDtypeStruct((depth_dev, LOCAL, PLANE), jnp.bfloat16),
            jax.ShapeDtypeStruct((27, rows, CH_IN), jnp.float32),
        ),
        in_specs=[vmem] * 4,
        out_specs=(vmem,) * 3,
        scratch_shapes=[
            pltpu.VMEM((4, 3, CH_IN, PLANE), jnp.bfloat16),
            pltpu.VMEM((4, 3, CH_OUT, PLANE), jnp.bfloat16),
            pltpu.VMEM((2, 4, CH_IN, HALO), jnp.bfloat16),
            pltpu.VMEM((2, 2, LOCAL, HALO), jnp.bfloat16),
            pltpu.VMEM((27, LOCAL, CH_IN), jnp.bfloat16),
            pltpu.VMEM((9, CH_OUT, HALO), jnp.bfloat16),
            pltpu.VMEM((2, 3 * LOCAL, PLANE), jnp.bfloat16),
            pltpu.VMEM((2, 2, 27, rows, half), jnp.float32),
            pltpu.VMEM((2, 27, rows, half), jnp.float32),
            pltpu.VMEM((27, rows, half), jnp.float32),
            pltpu.VMEM((27, rows, half), jnp.float32),
            pltpu.VMEM((27, rows, half), jnp.float32),
            pltpu.VMEM((27, rows, half), jnp.float32),
            pltpu.SemaphoreType.DMA((44,)),
            pltpu.SemaphoreType.DMA((44,)),
        ],
        compiler_params=pltpu.CompilerParams(
            collective_id=0, has_side_effects=True, vmem_limit_bytes=40 * 2**20
        ),
    )(
        jnp.transpose(activations, (1, 0, 2)),
        jnp.transpose(grad_out, (1, 0, 2)),
        weights,
        packed,
    )
    return (jnp.transpose(out, (1, 0, 2)), jnp.transpose(gin, (1, 0, 2)), fgrad)


def solution(mesh):
    paired = mesh.shape["filt"] == 2 * GROUPS and mesh.shape["slab"] == 2
    body = per_device_paired if paired else per_device_general
    in_specs = (P("filt", "slab", None), P("filt", "slab", None), P(None, "filt", None))
    out_specs = (P("filt", "slab", None), P("filt", "slab", None), P(None, "filt", None))
    return jax.shard_map(
        body, mesh=mesh, in_specs=in_specs, out_specs=out_specs, check_vma=False
    )
```

profile of v0, /device:TPU:5, one launch (start us, length us, event | category | flops | bytes accessed | tf_op | source)
XLA Modules:
  0.0 60.3 jit_solution(13613727670473139599)
XLA Ops:
  0.6 0.9 %copy_bitcast_fusion.1 = (bf16[2,32,512]{2,1,0:T(8,128)(2,1)S(1)}, bf16[2,32,512]{2,1,0:T(8,128)(2,1)S(1)}) fusion(bf16[32,2,512]{2,1,0:T(2,128)(2,1)} %param.4, bf16[32,2,512]{2,1,0:T(2,128)(2,1)} %param.3), kind=kLoop, calls=%fused_computation.1 | loop fusion | bytes 262144 | tf_op jit(solution)/shard_map/transpose | solution.py:383
  1.5 1.6 %reshape.12 = bf16[9,3,16,8,32]{4,3,2,1,0:T(8,128)(2,1)S(1)} reshape(bf16[27,16,256]{2,1,0:T(8,128)(2,1)} %refs_2_.1) | data formatting | bytes 442368 | tf_op jit(solution)/shard_map/reshape | solution.py:347
  3.1 0.8 %copy.19 = bf16[9,3,16,8,32]{4,1,2,0,3:T(4,128)(2,1)S(1)} copy(bf16[9,3,16,8,32]{4,3,2,1,0:T(8,128)(2,1)S(1)} %reshape.12) | data formatting | bytes 442368 | tf_op jit(solution)/shard_map/reshape | solution.py:347
  3.9 0.0 copy-start
  3.9 0.6 reshape.13
  4.5 0.1 pad.4.refs_3_
  4.5 0.3 copy-done
  4.8 53.3 %shard_map.58 = (bf16[2,32,512]{2,1,0:T(8,128)(2,1)S(1)}, bf16[2,32,512]{2,1,0:T(8,128)(2,1)S(1)}, f32[27,16,256]{2,1,0:T(8,128)S(1)}) custom-call(bf16[2,32,512]{2,1,0:T(8,128)(2,1)S(1)} %get-tuple-element.16.refs_0_, bf16[2,32,512]{2,1,0:T(8,128)(2,1)S(1)} %get-tuple-element.15.refs_1_, bf16[27,16,256]{2,1,0:T(8,128)(2,1)S(1)} %copy-done, ...), custom_call_target="tpu_custom_call" | custom-call | tf_op jit(solution)/shard_map/pallas_call | solution.py:352
  58.2 0.7 %copy.14 = bf16[32,2,512]{2,1,0:T(2,128)(2,1)} copy(bf16[32,2,512]{2,0,1:T(8,128)(2,1)S(1)} %bitcast.10) | data formatting | bytes 131072
  58.9 0.7 %copy.15 = bf16[32,2,512]{2,1,0:T(2,128)(2,1)} copy(bf16[32,2,512]{2,0,1:T(8,128)(2,1)S(1)} %bitcast.9) | data formatting | bytes 131072
  59.6 0.8 %copy.21 = f32[27,16,256]{2,1,0:T(8,128)} copy(f32[27,16,256]{2,1,0:T(8,128)S(1)} %get-tuple-element.22) | data formatting | bytes 884736
Async XLA Ops:
  3.9 0.9 %copy-start = (bf16[27,16,256]{2,1,0:T(8,128)(2,1)S(1)}, bf16[27,16,256]{2,1,0:T(8,128)(2,1)}, u32[]{:S(2)}) copy-start(bf16[27,16,256]{2,1,0:T(8,128)(2,1)} %refs_2_.1) | copy-start | bytes 663556
where the time goes:
time: 60.5 us; the launch traced here: 60.3 us
  Pallas kernels  53.3 us (88%)
  local copies, waits for them, and re-layouts  6.31 us (10%)
  between operations  0.68 us (1%)
    pallas_call x1, Pallas kernels, per_device_paired(): pl.pallas_call(lambda *refs: fused_kernel(1.0 / math.sqrt(cells), *refs),...  53.3 us
    unnamed x5, local copies, waits for them, and re-layouts  2.45 us
    reshape x2, local copies, waits for them, and re-layouts, per_device_paired(): weights.reshape(9, 3, rows, GROUPS, LOCAL)  2.35 us

commit v1 on v0

--- a/solution.py
+++ b/solution.py
@@ -156,8 +156,8 @@
 
 
 def fused_kernel(
-    scale, act, grad, own_w, own_wt, out, gin, fgrad,
-    vol_in, vol_grad, halo, halo_own, group_w, column_w, shifts,
+    scale, act, grad, own_w, out, gin, fgrad,
+    own_wt, vol_in, vol_grad, halo, halo_own, group_w, column_w, shifts,
     terms, terms_core, cross_out, cross_in, half_own, half_in,
     send, recv,
 ):
@@ -177,7 +177,9 @@
     def aligned(index, size):
         return pl.ds(pl.multiple_of(index * size, size), size)
 
-    peers = [block * GROUPS + (group + k) % GROUPS for k in range(1, GROUPS)]
+    quad, level = group % 4, group // 4
+    above = block * GROUPS + (1 - level) * 4 + quad
+    square = [block * GROUPS + level * 4 + (quad + k) % 4 for k in range(1, 4)]
     others = [(me + k) % (2 * GROUPS) for k in range(1, 2 * GROUPS)]
     barrier = pltpu.get_barrier_semaphore()
     for device in others:
@@ -188,30 +190,52 @@
     edge = pl.ds(pl.multiple_of((1 - block) * (PLANE - HALO), HALO), HALO)
     halo_own[0] = act[:, :, edge]
     halo_own[1] = grad[:, :, edge]
+    taps = own_w[...].reshape(9, 3, rows, CH_IN)
+    blank = jnp.zeros((9, rows, HALO - 3 * LOCAL), jnp.bfloat16)
+    for dest in range(GROUPS):
+        part = slice(dest * LOCAL, (dest + 1) * LOCAL)
+        own_wt[dest] = jnp.concatenate([taps[:, c, :, part] for c in range(3)] + [blank], axis=-1)
     pl.semaphore_wait(barrier, 2 * GROUPS)
+
+    channels_above = aligned((1 - level) * 4 + quad, LOCAL)
+
+    def spreading(src, view, first):
+        lift = remote(src, view(channels), first, above, slab)
+        near = [remote(src, view(channels), first + 1 + k, d, slab) for k, d in enumerate(square)]
+        passed = [
+            remote(view(channels_above), view(channels_above), first + 4 + k, d, slab)
+            for k, d in enumerate(square)
+        ]
+        return lift, near, passed
 
     halo_copy = remote(halo_own, halo.at[:, 1:3, channels, :], 0, across, slab)
     halo_copy.start()
-    act_copies = [
-        remote(act, vol_in.at[1:3, 1, channels, :], 8 + k, peer, slab)
-        for k, peer in enumerate(peers)
-    ]
-    for copy in act_copies:
-        copy.start()
-    group_copy = remote(own_w, group_w.at[:, aligned(block, rows), :], 22, across, slab)
+    act_lift, act_near, act_passed = spreading(act, lambda c: vol_in.at[1:3, 1, c, :], 8)
+    grad_lift, grad_near, grad_passed = spreading(grad, lambda c: vol_grad.at[1:3, 1, c, :], 15)
+    halo_lift, halo_near, halo_passed = spreading(
+        halo.at[:, 1:3, channels, :], lambda c: halo.at[:, 1:3, c, :], 1
+    )
+    act_lift.start()
+    for copy in act_near:
+        copy.start()
+    half = CH_IN // 2
+    side_lanes = aligned(slab, half)
+    group_copy = remote(
+        own_w.at[:, :, side_lanes], group_w.at[:, aligned(block, rows), side_lanes], 22, across, slab
+    )
     group_copy.start()
-    grad_copies = [
-        remote(grad, vol_grad.at[1:3, 1, channels, :], 15 + k, peer, slab)
-        for k, peer in enumerate(peers)
-    ]
-    for copy in grad_copies:
-        copy.start()
     mine = aligned(group * 2 + block, rows)
-    column_copies = [
-        remote(own_wt.at[device % GROUPS], column_w.at[:, mine, :], 23 + k, device, slab)
-        for k, device in enumerate(others)
-    ]
-    for copy in column_copies:
+    column_copies, column_passed = [], []
+    for k in range(1, GROUPS):
+        dest = (me + 2 * k + slab) % (2 * GROUPS)
+        column_copies.append(
+            remote(own_wt.at[dest % GROUPS], column_w.at[:, mine, :], 22 + k, dest, slab)
+        )
+        origin = (me + 2 * GROUPS - 2 * k - slab + 2 * GROUPS) % (2 * GROUPS)
+        theirs = column_w.at[:, aligned(origin % GROUPS * 2 + origin // GROUPS, rows), :]
+        column_passed.append(remote(theirs, theirs, 30 + k, me, other_slab))
+    column_next = remote(own_wt.at[others[0] % GROUPS], column_w.at[:, mine, :], 30, others[0], slab)
+    for copy in column_copies + [column_next]:
         copy.start()
 
     zero_plane = 3 * slab
@@ -232,22 +256,31 @@
         shifts[depth, 2 * LOCAL :] = upper.astype(jnp.bfloat16)
 
     halo_copy.wait_recv()
-    halo_copies = [
-        remote(halo.at[:, 1:3, channels, :], halo.at[:, 1:3, channels, :], 1 + k, peer, slab)
-        for k, peer in enumerate(peers)
-    ]
-    for copy in halo_copies:
+    halo_lift.start()
+    for copy in halo_near:
+        copy.start()
+    act_lift.wait_recv()
+    for copy in act_passed:
+        copy.start()
+    halo_lift.wait_recv()
+    for copy in halo_passed:
+        copy.start()
+    grad_lift.start()
+    for copy in grad_near:
         copy.start()
 
     gives, takes = 2 - slab, 3 * slab
-    for copy in act_copies:
+    for copy in act_near + act_passed:
         copy.wait_recv()
     act_plane = remote(vol_in.at[gives, 1], vol_in.at[takes, 1], 38, me, other_slab)
     act_plane.start()
-    for copy in halo_copies:
+    for copy in halo_near + halo_passed:
         copy.wait_recv()
     halo_plane = remote(halo.at[:, gives], halo.at[:, takes], 39, me, other_slab)
     halo_plane.start()
+    grad_lift.wait_recv()
+    for copy in grad_passed:
+        copy.start()
 
     def shift_rows(volume, which, plane):
         edges = halo[which, plane]
@@ -267,26 +300,48 @@
     shift_rows(vol_in, 0, 3)
 
     over_cells = (((1,), (1,)), ((), ()))
-    half = CH_IN // 2
-    for pair in range(9):
-        a, b = pair // 3, pair % 3
-        total = sum(
-            lax.dot_general(
-                shifts[depth], vol_in[depth + a, b], over_cells, preferred_element_type=jnp.float32
+    def part(a):
+        return pl.ds(9 * a, 9)
+
+    terms_copies = [
+        remote(terms.at[other_slab, :, part(a)], terms_core.at[:, part(a)], 41 + a, me, other_slab)
+        for a in range(3)
+    ]
+    crossing = [
+        remote(cross_out.at[part(a)], cross_in.at[part(a)], 45 + a, across, slab) for a in range(3)
+    ]
+
+    def cross(a):
+        terms_copies[a].wait_recv()
+        cross_out[part(a)] = terms[slab, 1 - block, part(a)] + terms_core[1 - block, part(a)]
+        crossing[a].start()
+
+    for a in range(3):
+        for b in range(3):
+            total = sum(
+                lax.dot_general(
+                    shifts[depth], vol_in[depth + a, b], over_cells,
+                    preferred_element_type=jnp.float32,
+                )
+                for depth in range(2)
             )
-            for depth in range(2)
-        )
-        for c in range(3):
-            for dest in range(2):
-                low = c * LOCAL + dest * rows
-                for side in range(2):
-                    terms[side, dest, 3 * pair + c] = total[
-                        low : low + rows, side * half : (side + 1) * half
-                    ]
-    terms_copy = remote(terms.at[other_slab], terms_core, 41, me, other_slab)
-    terms_copy.start()
+            for c in range(3):
+                for dest in range(2):
+                    low = c * LOCAL + dest * rows
+                    for side in range(2):
+                        terms[side, dest, 9 * a + 3 * b + c] = total[
+                            low : low + rows, side * half : (side + 1) * half
+                        ]
+        terms_copies[a].start()
+        if a > 0:
+            cross(a - 1)
 
     group_copy.wait_recv()
+    arrived = group_w.at[:, aligned(1 - block, rows), side_lanes]
+    group_passed = remote(arrived, arrived, 44, me, other_slab)
+    group_passed.start()
+    cross(2)
+    group_passed.wait_recv()
     for depth in range(2):
         total = jnp.zeros((3 * LOCAL, PLANE), jnp.float32)
         for pair in range(9):
@@ -296,12 +351,10 @@
             )
         out[depth] = spread(total, True).astype(out.dtype)
 
-    terms_copy.wait_recv()
-    cross_out[...] = terms[slab, 1 - block] + terms_core[1 - block]
-    cross = remote(cross_out, cross_in, 42, across, slab)
-    cross.start()
-
-    for copy in grad_copies:
+    for copy, onward in zip(column_copies, column_passed):
+        copy.wait_recv()
+        onward.start()
+    for copy in grad_near + grad_passed:
         copy.wait_recv()
     grad_plane = remote(vol_grad.at[gives, 1], vol_grad.at[takes, 1], 40, me, other_slab)
     grad_plane.start()
@@ -310,7 +363,7 @@
     grad_plane.wait_recv()
     shift_rows(vol_grad, 1, 0)
     shift_rows(vol_grad, 1, 3)
-    for copy in column_copies:
+    for copy in column_passed + [column_next]:
         copy.wait_recv()
     over_rows = (((0,), (0,)), ((), ()))
     totals = [jnp.zeros((HALO, PLANE), jnp.float32) for _ in range(2)]
@@ -324,17 +377,24 @@
     for depth in range(2):
         gin[depth] = spread(totals[depth], False).astype(gin.dtype)
 
-    cross.wait_recv()
-    half_own[...] = (terms[slab, block] + terms_core[block] + cross_in[...]) * scale
-    share = remote(half_own, half_in, 43, me, other_slab)
-    share.start()
-    fgrad[:, :, aligned(slab, half)] = half_own[...]
-    share.wait_recv()
+    shares = [
+        remote(half_own.at[part(a)], half_in.at[part(a)], 48 + a, me, other_slab) for a in range(3)
+    ]
+    for a in range(3):
+        crossing[a].wait_recv()
+        mean = (terms[slab, block, part(a)] + terms_core[block, part(a)] + cross_in[part(a)]) * scale
+        half_own[part(a)] = mean
+        shares[a].start()
+        fgrad[part(a), :, side_lanes] = mean
+    for copy in shares:
+        copy.wait_recv()
     fgrad[:, :, aligned(other_slab, half)] = half_in[...]
 
     for copy in (
-        [halo_copy, group_copy, act_plane, halo_plane, grad_plane, terms_copy, cross, share]
-        + halo_copies + act_copies + grad_copies + column_copies
+        [halo_copy, group_copy, group_passed, act_plane, halo_plane, grad_plane, column_next]
+        + [act_lift, grad_lift, halo_lift]
+        + act_near + act_passed + grad_near + grad_passed + halo_near + halo_passed
+        + column_copies + column_passed + terms_copies + crossing + shares
     ):
         copy.wait_send()
 
@@ -343,10 +403,6 @@
     depth_dev = activations.shape[1]
     rows = weights.shape[1]
     cells = depth_dev * 2 * ROWS * 2 * WIDTH
-    packed = jnp.transpose(
-        weights.reshape(9, 3, rows, GROUPS, LOCAL), (3, 0, 2, 1, 4)
-    ).reshape(GROUPS, 9, rows, 3 * LOCAL)
-    packed = jnp.pad(packed, ((0, 0), (0, 0), (0, 0), (0, HALO - 3 * LOCAL)))
     vmem = pl.BlockSpec(memory_space=pltpu.VMEM)
     half = CH_IN // 2
     out, gin, fgrad = pl.pallas_call(
@@ -356,9 +412,10 @@
             jax.ShapeDtypeStruct((depth_dev, LOCAL, PLANE), jnp.bfloat16),
             jax.ShapeDtypeStruct((27, rows, CH_IN), jnp.float32),
         ),
-        in_specs=[vmem] * 4,
+        in_specs=[vmem] * 3,
         out_specs=(vmem,) * 3,
         scratch_shapes=[
+            pltpu.VMEM((GROUPS, 9, rows, HALO), jnp.bfloat16),
             pltpu.VMEM((4, 3, CH_IN, PLANE), jnp.bfloat16),
             pltpu.VMEM((4, 3, CH_OUT, PLANE), jnp.bfloat16),
             pltpu.VMEM((2, 4, CH_IN, HALO), jnp.bfloat16),
@@ -372,8 +429,8 @@
             pltpu.VMEM((27, rows, half), jnp.float32),
             pltpu.VMEM((27, rows, half), jnp.float32),
             pltpu.VMEM((27, rows, half), jnp.float32),
-            pltpu.SemaphoreType.DMA((44,)),
-            pltpu.SemaphoreType.DMA((44,)),
+            pltpu.SemaphoreType.DMA((51,)),
+            pltpu.SemaphoreType.DMA((51,)),
         ],
         compiler_params=pltpu.CompilerParams(
             collective_id=0, has_side_effects=True, vmem_limit_bytes=40 * 2**20
@@ -382,7 +439,6 @@
         jnp.transpose(activations, (1, 0, 2)),
         jnp.transpose(grad_out, (1, 0, 2)),
         weights,
-        packed,
     )
     return (jnp.transpose(out, (1, 0, 2)), jnp.transpose(gin, (1, 0, 2)), fgrad)
 

time: 60.5 us -> 42.1 us (0.70)
  the two profiles are of different devices: /device:TPU:5 before, /device:TPU:0 now
where the time goes in v1:
time: 42.1 us; the launch traced here: 41.9 us
  Pallas kernels  38.1 us (90%)
  local copies, waits for them, and re-layouts  3.14 us (7%)
  between operations  0.65 us (2%)
    pallas_call x1, Pallas kernels, per_device_paired(): pl.pallas_call(lambda *refs: fused_kernel(1.0 / math.sqrt(cells), *refs),...  38.1 us
    unnamed x5, local copies, waits for them, and re-layouts  2.22 us
    transpose x1, local copies, waits for them, and re-layouts, per_device_paired(): jnp.transpose(grad_out, (1, 0, 2))  0.93 us

profile of v1, /device:TPU:0, one launch (start us, length us, event | category | flops | bytes accessed | tf_op | source)
XLA Modules:
  0.0 41.9 jit_solution(1813828085030842037)
XLA Ops:
  0.6 0.0 copy-start
  0.6 0.9 %copy_bitcast_fusion = (bf16[2,32,512]{2,1,0:T(8,128)(2,1)S(1)}, bf16[2,32,512]{2,1,0:T(8,128)(2,1)S(1)}) fusion(bf16[32,2,512]{2,1,0:T(2,128)(2,1)} %param.4, bf16[32,2,512]{2,1,0:T(2,128)(2,1)} %param.3), kind=kLoop, calls=%fused_computation | loop fusion | bytes 262144 | tf_op jit(solution)/shard_map/transpose | solution.py:440
  1.6 0.1 copy-done
  1.6 38.1 %shard_map.58 = (bf16[2,32,512]{2,1,0:T(8,128)(2,1)S(1)}, bf16[2,32,512]{2,1,0:T(8,128)(2,1)S(1)}, f32[27,16,256]{2,1,0:T(8,128)S(1)}) custom-call(bf16[2,32,512]{2,1,0:T(8,128)(2,1)S(1)} %get-tuple-element.13.refs_0_, bf16[2,32,512]{2,1,0:T(8,128)(2,1)S(1)} %get-tuple-element.12.refs_1_, bf16[27,16,256]{2,1,0:T(8,128)(2,1)S(1)} %copy-done), custom_call_target="tpu_custom_call" | custom-call | tf_op jit(solution)/shard_map/pallas_call | solution.py:408
  39.8 0.7 %copy.8 = bf16[32,2,512]{2,1,0:T(2,128)(2,1)} copy(bf16[32,2,512]{2,0,1:T(8,128)(2,1)S(1)} %bitcast.7) | data formatting | bytes 131072
  40.5 0.7 %copy.9 = bf16[32,2,512]{2,1,0:T(2,128)(2,1)} copy(bf16[32,2,512]{2,0,1:T(8,128)(2,1)S(1)} %bitcast.6) | data formatting | bytes 131072
  41.2 0.8 %copy.13 = f32[27,16,256]{2,1,0:T(8,128)} copy(f32[27,16,256]{2,1,0:T(8,128)S(1)} %get-tuple-element.19) | data formatting | bytes 884736
Async XLA Ops:
  0.6 1.0 %copy-start = (bf16[27,16,256]{2,1,0:T(8,128)(2,1)S(1)}, bf16[27,16,256]{2,1,0:T(8,128)(2,1)}, u32[]{:S(2)}) copy-start(bf16[27,16,256]{2,1,0:T(8,128)(2,1)} %refs_2_.1) | copy-start | bytes 663556

commit v2 on v1

--- a/solution.py
+++ b/solution.py
@@ -218,6 +218,7 @@
     act_lift.start()
     for copy in act_near:
         copy.start()
+    grad_lift.start()
     half = CH_IN // 2
     side_lanes = aligned(slab, half)
     group_copy = remote(
@@ -235,8 +236,6 @@
         theirs = column_w.at[:, aligned(origin % GROUPS * 2 + origin // GROUPS, rows), :]
         column_passed.append(remote(theirs, theirs, 30 + k, me, other_slab))
     column_next = remote(own_wt.at[others[0] % GROUPS], column_w.at[:, mine, :], 30, others[0], slab)
-    for copy in column_copies + [column_next]:
-        copy.start()
 
     zero_plane = 3 * slab
     vol_in[zero_plane, 1] = jnp.zeros((CH_IN, PLANE), jnp.bfloat16)
@@ -265,8 +264,9 @@
     halo_lift.wait_recv()
     for copy in halo_passed:
         copy.start()
-    grad_lift.start()
     for copy in grad_near:
+        copy.start()
+    for copy in column_copies + [column_next]:
         copy.start()
 
     gives, takes = 2 - slab, 3 * slab

time: 42.1 us -> 41 us (0.974)
  Pallas kernels: 38.1 us -> 37 us
    pallas_call x1, Pallas kernels: 38.1 us -> 37 us  [per_device_paired(): pl.pallas_call(lambda *refs: fused_kernel(1.0 / math.sqrt(cells), *refs),...]
where the time goes in v2:
time: 41 us; the launch traced here: 40.8 us
  Pallas kernels  37 us (90%)
  local copies, waits for them, and re-layouts  3.14 us (8%)
  between operations  0.65 us (2%)
    pallas_call x1, Pallas kernels, per_device_paired(): pl.pallas_call(lambda *refs: fused_kernel(1.0 / math.sqrt(cells), *refs),...  37 us
    unnamed x5, local copies, waits for them, and re-layouts  2.22 us
    transpose x1, local copies, waits for them, and re-layouts, per_device_paired(): jnp.transpose(grad_out, (1, 0, 2))  0.93 us

profile of v2, /device:TPU:0, one launch (start us, length us, event | category | flops | bytes accessed | tf_op | source)
XLA Modules:
  0.0 40.8 jit_solution(12045598643854236280)
XLA Ops:
  0.6 0.0 copy-start
  0.6 0.9 %copy_bitcast_fusion = (bf16[2,32,512]{2,1,0:T(8,128)(2,1)S(1)}, bf16[2,32,512]{2,1,0:T(8,128)(2,1)S(1)}) fusion(bf16[32,2,512]{2,1,0:T(2,128)(2,1)} %param.4, bf16[32,2,512]{2,1,0:T(2,128)(2,1)} %param.3), kind=kLoop, calls=%fused_computation | loop fusion | bytes 262144 | tf_op jit(solution)/shard_map/transpose | solution.py:440
  1.6 0.1 copy-done
  1.6 37.0 %shard_map.58 = (bf16[2,32,512]{2,1,0:T(8,128)(2,1)S(1)}, bf16[2,32,512]{2,1,0:T(8,128)(2,1)S(1)}, f32[27,16,256]{2,1,0:T(8,128)S(1)}) custom-call(bf16[2,32,512]{2,1,0:T(8,128)(2,1)S(1)} %get-tuple-element.13.refs_0_, bf16[2,32,512]{2,1,0:T(8,128)(2,1)S(1)} %get-tuple-element.12.refs_1_, bf16[27,16,256]{2,1,0:T(8,128)(2,1)S(1)} %copy-done), custom_call_target="tpu_custom_call" | custom-call | tf_op jit(solution)/shard_map/pallas_call | solution.py:408
  38.6 0.7 %copy.8 = bf16[32,2,512]{2,1,0:T(2,128)(2,1)} copy(bf16[32,2,512]{2,0,1:T(8,128)(2,1)S(1)} %bitcast.7) | data formatting | bytes 131072
  39.3 0.7 %copy.9 = bf16[32,2,512]{2,1,0:T(2,128)(2,1)} copy(bf16[32,2,512]{2,0,1:T(8,128)(2,1)S(1)} %bitcast.6) | data formatting | bytes 131072
  40.0 0.8 %copy.13 = f32[27,16,256]{2,1,0:T(8,128)} copy(f32[27,16,256]{2,1,0:T(8,128)S(1)} %get-tuple-element.19) | data formatting | bytes 884736
Async XLA Ops:
  0.6 1.0 %copy-start = (bf16[27,16,256]{2,1,0:T(8,128)(2,1)S(1)}, bf16[27,16,256]{2,1,0:T(8,128)(2,1)}, u32[]{:S(2)}) copy-start(bf16[27,16,256]{2,1,0:T(8,128)(2,1)} %refs_2_.1) | copy-start | bytes 663556
